TPU v7x, 128 devices: a whole 4x4x4 slice. The times are simulated.
128 devices in a mesh: band: 8 (over z_hi, x), gvec: 16 (over y, z_lo, core).
Axes of the slice: x: 4, y: 4, z: 4 (z_hi: 2, z_lo: 2; z = z_hi * 2 + z_lo), core: 2. Of those that a mesh axis runs over, the one named last changes fastest.
Arguments:
- coeffs: bfloat16 [131072, 1024], P('gvec', 'band'), may hold values from -6 to 6
- rotation: bfloat16 [1024, 4096], P('gvec', 'band'), may hold values from -0.1875 to 0.1875
Outputs:
- rotated: bfloat16 [131072, 4096], P('gvec', 'band')
All inputs are finite; a program needn't handle non-finite values.
Results may differ from a plain program's by a relative error of at most 0.001.
Values may be sent and summed in bfloat16 or wider, within the bound.
A program may use at most 128 MiB of HBM per device.

v0:
```python
import jax
import jax.numpy as jnp
from jax import lax
from jax.sharding import PartitionSpec as P


def on_device(coeffs, rotation):
    rows_full = lax.all_gather(rotation, "gvec", axis=0, tiled=True)
    whole = lax.all_gather(coeffs, "band", axis=1, tiled=True)
    total = jnp.dot(whole, rows_full, preferred_element_type=jnp.float32)
    return total.astype(jnp.bfloat16)


def solution(mesh):
    return jax.shard_map(
        on_device,
        mesh=mesh,
        in_specs=(P("gvec", "band"), P("gvec", "band")),
        out_specs=P("gvec", "band"),
        check_vma=False,
    )
```

profile of v0, /device:TPU:0, one launch (start us, length us, event | category | flops | bytes accessed | tf_op | source)
XLA Modules:
  0.0 274.0 jit_solution(17764802183526045215)
XLA Ops:
  6.5 0.0 all-gather.5.cloned.1.call-start
  6.5 0.7 all-gather.5.cloned.1.call-update
  7.3 0.0 all-gather.3.cloned.1.call-start
  7.3 0.7 all-gather.3.cloned.1.call-update
  8.0 36.1 %all-gather.5.cloned.1.call-done = bf16[1024,512]{1,0:T(8,128)(2,1)} async-done(((bf16[64,512]{1,0:T(8,128)(2,1)}), bf16[1024,512]{1,0:T(8,128)(2,1)}) %all-gather.5.cloned.1.call-update) | async-done | bytes 1048592 | tf_op jit(solution)/shard_map/all_gather | solution.py:8
  44.1 208.4 %all-gather.3.cloned.1.call-done = bf16[8192,1024]{1,0:T(8,128)(2,1)} async-done(((bf16[8192,128]{1,0:T(8,128)(2,1)}), bf16[8192,1024]{1,0:T(8,128)(2,1)}) %all-gather.3.cloned.1.call-update) | async-done | bytes 16777232 | tf_op jit(solution)/shard_map/all_gather | solution.py:9
  252.4 14.7 %convolution_convert_fusion = bf16[8192,512]{1,0:T(8,128)(2,1)} fusion(bf16[8192,1024]{1,0:T(8,128)(2,1)} %all-gather.3.cloned.1.call-done, bf16[1024,512]{1,0:T(8,128)(2,1)} %all-gather.5.cloned.1.call-done), kind=kOutput, calls=%fused_computation | convolution fusion | flops 8594128896 | bytes 26214400 | tf_op jit(solution)/shard_map/dot_general | solution.py:10
Async XLA Ops:
  6.5 37.5 %all-gather.5.cloned.1.call-start = ((), (), s32[]{:S(2)}) async-start(), calls=%async_computation.1 | async-start | bytes 1114112 | tf_op jit(solution)/shard_map/all_gather | solution.py:8
  7.3 245.2 %all-gather.3.cloned.1.call-start = ((), (), s32[]{:S(2)}) async-start(), calls=%async_computation | async-start | bytes 18874368 | tf_op jit(solution)/shard_map/all_gather | solution.py:9
Sparse Core Ops, SparseCore 0:
  9.1 34.9 all-gather.4
  46.2 206.1 all-gather.2
where the time goes:
time: 274 us
  waiting for transfers between devices  246 us (90%)
  matrix products  14.7 us (5%)
  between operations  13.4 us (5%)
    all_gather x1, waiting for transfers between devices, on_device(): whole = lax.all_gather(coeffs, 'band', axis=1, tiled=True)  208 us
    all_gather x1, waiting for transfers between devices, on_device(): rows_full = lax.all_gather(rotation, 'gvec', axis=0, tiled=True)  36.1 us
    dot_general x1, matrix products, on_device(): total = jnp.dot(whole, rows_full, preferred_element_type=jnp.float32)  14.7 us
  transfers between devices with their start and end apart: 2, of which 2 were waited for; matrix products, arithmetic and copies ran while one was open for 0% of the time, Pallas kernels for 0%

commit v1 on v0

v1 whole, which is shorter than its diff:
```python
import functools

import jax
import jax.numpy as jnp
from jax import lax
from jax.experimental import pallas as pl
from jax.experimental.pallas import tpu as pltpu
from jax.sharding import PartitionSpec as P

MESH = pl.DeviceIdType.MESH
R = 256
AHEAD = 2
START = 4


def kernel(nb, n, coef, rot, out, gath, full, prod, *sems):
    (own_s, own_r, par_s, par_r, fwd_s, fwd_r, k_s, k_r, p_s, p_r, z_s, z_r, y_s, y_r, c_s, c_r, loc) = sems
    half = R // 2
    band, gvec = lax.axis_index("band"), lax.axis_index("gvec")
    x, zh = lax.rem(band, 4), band // 4
    y, zl, c = gvec // 4, lax.rem(gvec // 2, 2), lax.rem(gvec, 2)
    xp, xm = lax.rem(x + 1, 4), lax.rem(x + 3, 4)
    oh = 1 - zh

    def at(x_=x, y_=y, zh_=zh, zl_=zl, c_=c):
        return (zh_ * 4 + x_, y_ * 4 + zl_ * 2 + c_)

    right, left, across = at(x_=xp), at(x_=xm), at(zh_=oh)
    z_peers = (at(zl_=1 - zl), at(zh_=oh, zl_=1 - zl), across)
    y_peers = tuple(at(y_=lax.rem(y + d, 4)) for d in (1, 3, 2))
    twin = at(c_=1 - c)

    def send(src, dst, s, r, dev):
        return pltpu.make_async_remote_copy(src_ref=src, dst_ref=dst, send_sem=s, recv_sem=r, device_id=dev, device_id_type=MESH)

    def row(i, plane):
        return pl.multiple_of(jnp.where(i < nb, plane * nb + i, nb + i) * R, R)

    def own(i, d):
        rows = pl.ds(row(i, zh), R)
        return send(coef.at[rows], gath.at[x, zh, rows], own_s.at[d, i], own_r.at[d, i], (right, left)[d])

    def partner(i, d):
        ref = gath.at[x, oh, pl.ds(row(i, zh), R)]
        return send(ref, ref, par_s.at[d, i], par_r.at[d, i], (right, left)[d])

    def forward(i, d):
        ref = gath.at[(xm, xp)[d], :, pl.ds(row(i, zh) + d * half, half)]
        return send(ref, ref, fwd_s.at[d, i], fwd_r.at[d, i], (right, left)[d])

    def over(i):
        rows = pl.ds(row(i, oh), R)
        return send(coef.at[rows], gath.at[x, zh, rows], k_s.at[i], k_r.at[i], across)

    def product(i):
        return send(prod.at[pl.ds(i * R, R)], out.at[pl.ds(row(i, zh), R)], p_s.at[i], p_r.at[i], across)

    def compute(i):
        for d in range(2):
            forward(i, d).wait_recv()
        rows = pl.ds(row(i, zh), R)

        def times(columns):
            lhs = jnp.concatenate([gath[b % 4, b // 4, rows, :] for b in range(8)], axis=1)
            rhs = full[columns].reshape(1024, full.shape[-1])
            return jnp.dot(lhs, rhs, preferred_element_type=jnp.float32).astype(out.dtype)

        @pl.when(i < nb)
        def _():
            prod[pl.ds(i * R, R), :] = times(oh)
            product(i).start()

        out[rows, :] = times(zh)

    mine = full.at[zh, y, zl, c]
    z_sends = [send(rot, mine, z_s.at[k], z_r.at[k], dev) for k, dev in enumerate(z_peers)]
    line = full.at[:, y, :, c]
    y_sends = [send(line, line, y_s.at[k], y_r.at[k], dev) for k, dev in enumerate(y_peers)]
    plane = full.at[:, :, :, c]
    c_send = send(plane, plane, c_s, c_r, twin)

    local_rot = pltpu.make_async_copy(rot, mine, loc.at[0])
    local_coef = pltpu.make_async_copy(coef, gath.at[x, zh], loc.at[1])

    peers = (right, left, *z_peers, *y_peers, twin)
    barrier = pltpu.get_barrier_semaphore()
    for dev in peers:
        pl.semaphore_signal(barrier, inc=1, device_id=dev, device_id_type=MESH)
    local_rot.start()
    pl.semaphore_wait(barrier, len(peers))

    over(0).start()
    for i in range(AHEAD):
        for d in range(2):
            own(i, d).start()
    for s in z_sends:
        s.start()

    @pl.loop(1, n)
    def _(i):
        over(i).start()

    local_coef.start()
    local_rot.wait()
    local_coef.wait()

    def begin(t):
        return jnp.maximum(0, jnp.minimum(2 * (t - START), t - 2))

    @pl.loop(0, n + 2)
    def _(t):
        @pl.when(t + AHEAD < n)
        def _():
            for d in range(2):
                own(t + AHEAD, d).start()

        @pl.when(t < n)
        def _():
            over(t).wait_recv()
            for d in range(2):
                partner(t, d).start()

        @pl.when(jnp.logical_and(t >= 1, t < n + 1))
        def _():
            for d in range(2):
                own(t - 1, d).wait_recv()
                partner(t - 1, d).wait_recv()
                forward(t - 1, d).start()

        @pl.when(t == 1)
        def _():
            for s in z_sends:
                s.wait()
            for s in y_sends:
                s.start()

        @pl.when(t == START - 1)
        def _():
            for s in y_sends:
                s.wait()
            c_send.start()

        @pl.when(t == START)
        def _():
            c_send.wait()

        @pl.loop(begin(t), begin(t + 1))
        def _(i):
            compute(i)

    @pl.loop(0, nb)
    def _(i):
        product(i).wait()

    @pl.loop(0, n)
    def _(i):
        over(i).wait_send()
        for d in range(2):
            own(i, d).wait_send()
            partner(i, d).wait_send()
            forward(i, d).wait_send()


def on_device(coeffs, rotation):
    rows, depth = coeffs.shape
    columns = rotation.shape[1]
    nb = rows // R // 3
    n = rows // R - nb
    dma = pltpu.SemaphoreType.DMA
    return pl.pallas_call(
        functools.partial(kernel, nb, n),
        out_shape=jax.ShapeDtypeStruct((rows, columns), coeffs.dtype),
        in_specs=[pl.BlockSpec(memory_space=pl.ANY)] * 2,
        out_specs=pl.BlockSpec(memory_space=pltpu.VMEM),
        scratch_shapes=[
            pltpu.VMEM((4, 2, rows, depth), coeffs.dtype),
            pltpu.VMEM((2, 4, 2, 2, rotation.shape[0], columns), coeffs.dtype),
            pltpu.VMEM((nb * R, columns), coeffs.dtype),
            dma((2, n)), dma((2, n)), dma((2, n)), dma((2, n)), dma((2, n)), dma((2, n)),
            dma((n,)), dma((n,)), dma((nb,)), dma((nb,)),
            dma((3,)), dma((3,)), dma((3,)), dma((3,)), dma, dma, dma((2,)),
        ],
        compiler_params=pltpu.CompilerParams(
            collective_id=0, has_side_effects=True, vmem_limit_bytes=56 * 2**20
        ),
        cost_estimate=pl.CostEstimate(flops=2 * rows * 1024 * columns, bytes_accessed=rows * columns * 2, transcendentals=0),
    )(coeffs, rotation)


def solution(mesh):
    return jax.shard_map(
        on_device,
        mesh=mesh,
        in_specs=(P("gvec", "band"), P("gvec", "band")),
        out_specs=P("gvec", "band"),
        check_vma=False,
    )
```

time: 274 us -> 121 us (0.44)
  waiting for transfers between devices: 246 us -> 0 us
  Pallas kernels: 0 us -> 113 us
  matrix products: 14.7 us -> 0 us
  between operations: 13.4 us -> 0.01 us
  local copies, waits for them, and re-layouts: 0 us -> 7.32 us
    all_gather x2 -> x0, waiting for transfers between devices: 244 us -> none  [the longest x1 208 us: on_device(): whole = lax.all_gather(coeffs, 'band', axis=1, tiled=True)]
    pallas_call x0 -> x1, Pallas kernels: none -> 113 us  [on_device(): pl.pallas_call(functools.partial(kernel, nb, n), out_shape=jax.ShapeDtype...]
    dot_general x1 -> x0, matrix products: 14.7 us -> none  [on_device(): total = jnp.dot(whole, rows_full, preferred_element_type=jnp.float32)]
    unnamed x0 -> x1, local copies, waits for them, and re-layouts: none -> 7.32 us
  transfers between devices with their start and end apart: 2 -> 0, of which waited for: 2 -> 0; matrix products, arithmetic and copies ran while one was open for 0% -> 0% of each run, Pallas kernels for 0% -> 0%
where the time goes in v1:
time: 121 us; the launch traced here: 120 us
  Pallas kernels  113 us (93%)
  local copies, waits for them, and re-layouts  7.32 us (6%)
    pallas_call x1, Pallas kernels, on_device(): pl.pallas_call(functools.partial(kernel, nb, n), out_shape=jax.ShapeDtype...  113 us
    unnamed x1, local copies, waits for them, and re-layouts  7.32 us

profile of v1, /device:TPU:0, one launch (start us, length us, event | category | flops | bytes accessed | tf_op | source)
XLA Modules:
  0.0 120.4 jit_solution(12825542848053505415)
XLA Ops:
  0.0 113.0 %shard_map.28 = bf16[8192,512]{1,0:T(8,128)(2,1)} custom-call(bf16[8192,128]{1,0:T(8,128)(2,1)} %coef.1, bf16[64,512]{1,0:T(8,128)(2,1)} %rot.1), custom_call_target="tpu_custom_call" | custom-call | flops 8589934592 | bytes 8388608 | tf_op jit(solution)/shard_map/pallas_call | solution.py:170
  113.1 7.3 %copy.4 = bf16[8192,512]{1,0:T(8,128)(2,1)} copy(bf16[8192,512]{1,0:T(8,128)(2,1)} %shard_map.28) | data formatting | bytes 16777216

commit v2 on v0

v2 whole, which is shorter than its diff:
```python
import functools

import jax
import jax.numpy as jnp
from jax import lax
from jax.experimental import pallas as pl
from jax.experimental.pallas import tpu as pltpu
from jax.sharding import PartitionSpec as P

MESH = pl.DeviceIdType.MESH
R = 128
NJ = 7
K_AHEAD, OWN_AHEAD = 6, 4
L_PARTNER, L_FORWARD, L_MULTIPLY = 3, 6, 9
FIRST_MATE, FIRST_PAIR = 6, 11
ROT_1, ROT_2, ROT_3, START, ROT_4, ROT_5 = 2, 4, 6, 7, 9, 10


def kernel(nb, nj, coef, rot, out, gath, full, prod, jprod, *sems):
    (own_s, own_r, par_s, par_r, fwd_s, fwd_r, k_s, k_r, p_s, p_r,
     feed_s, feed_r, jk_s, jk_r, jf_s, jf_r, ma_s, ma_r, mb_s, mb_r, jo_s, jo_r,
     z_s, z_r, x_s, x_r, y_s, y_r, c_s, c_r, loc) = sems
    half = R // 2
    band, gvec = lax.axis_index("band"), lax.axis_index("gvec")
    x, zh = lax.rem(band, 4), band // 4
    y, zl, c = gvec // 4, lax.rem(gvec // 2, 2), lax.rem(gvec, 2)
    xp, xm, x2 = lax.rem(x + 1, 4), lax.rem(x + 3, 4), lax.rem(x + 2, 4)
    oh = 1 - zh

    def at(x_=x, y_=y, zh_=zh, zl_=zl, c_=c):
        return (zh_ * 4 + x_, y_ * 4 + zl_ * 2 + c_)

    right, left, across = at(x_=xp), at(x_=xm), at(zh_=oh)
    ways = (right, left)
    z_peers = (at(zl_=1 - zl), across, at(zh_=oh, zl_=1 - zl))
    y_peers = tuple(at(y_=lax.rem(y + d, 4)) for d in (1, 3, 2))
    twin = at(c_=1 - c)

    def send(src, dst, s, r, dev):
        return pltpu.make_async_remote_copy(src_ref=src, dst_ref=dst, send_sem=s, recv_sem=r, device_id=dev, device_id_type=MESH)


    def rows_of(i, plane):
        return pl.ds(pl.multiple_of((plane * nb + i) * R, R), R)

    def own(i, d):
        rows = rows_of(i, zh)
        return send(coef.at[rows], gath.at[x, zh, rows], own_s.at[d], own_r.at[d, i], ways[d])

    def partner(i, d):
        ref = gath.at[x, oh, rows_of(i, zh)]
        return send(ref, ref, par_s.at[d], par_r.at[d, i], ways[d])

    def forward(i, d):
        ref = gath.at[(xm, xp)[d], :, pl.ds(pl.multiple_of((zh * nb + i) * R + d * half, half), half)]
        return send(ref, ref, fwd_s.at[d], fwd_r.at[d, i], ways[d])

    def over(i):
        rows = rows_of(i, oh)
        return send(coef.at[rows], gath.at[x, zh, rows], k_s, k_r.at[i], across)

    def product(i):
        return send(prod.at[pl.ds(i * R, R)], out.at[rows_of(i, zh)], p_s, p_r, across)


    pair = (x, xm)
    feeder = (xm, xp)
    fed = (xp, x2)

    def pair_rows(i, j):
        return pl.ds(pl.multiple_of((2 * nb + j * nj + i) * R, R), R)

    def feed(i, d):
        rows = pair_rows(i, fed[d])
        return send(coef.at[rows], gath.at[x, zh, rows], feed_s.at[d], feed_r.at[d, i], ways[d])

    def pair_over(i, d):
        rows = pair_rows(i, pair[d])
        return send(coef.at[rows], gath.at[x, zh, rows], jk_s.at[d], jk_r.at[d, i], across)

    def feeder_over(i, d):
        ref = gath.at[feeder[d], zh, pair_rows(i, pair[d])]
        return send(ref, ref, jf_s.at[d], jf_r.at[d, i], across)

    def mate_own(i, d):
        ref = gath.at[x, :, pair_rows(i, pair[d])]
        return send(ref, ref, ma_s.at[d], ma_r.at[d, i], ways[d])

    def mate_fed(i, d):
        ref = gath.at[feeder[d], :, pair_rows(i, pair[d])]
        return send(ref, ref, mb_s.at[d], mb_r.at[d, i], ways[d])

    def pair_product(i, d):
        return send(jprod.at[d, pl.ds(i * R, R)], out.at[pair_rows(i, pair[d])], jo_s.at[d], jo_r.at[d], ways[1 - d])


    z_sends = [send(rot, full.at[(0, 1, 1)[k], y, zl, c], z_s.at[k], z_r.at[k], dev) for k, dev in enumerate(z_peers)]
    x_sends = [send(full.at[0, y, :, c], full.at[2 + d, y, :, c], x_s.at[d], x_r.at[d], ways[d]) for d in range(2)]

    def y_sends(g):
        ref = full.at[2 * g : 2 * g + 2, y, :, c]
        return [send(ref, ref, y_s.at[g, k], y_r.at[g, k], dev) for k, dev in enumerate(y_peers)]

    def c_send(g):
        ref = full.at[2 * g : 2 * g + 2, :, :, c]
        return send(ref, ref, c_s.at[g], c_r.at[g], twin)

    def times(rows, columns):
        lhs = jnp.concatenate([gath[b % 4, b // 4, rows, :] for b in range(8)], axis=1)
        rhs = full[columns].reshape(1024, full.shape[-1])
        return jnp.dot(lhs, rhs, preferred_element_type=jnp.float32).astype(out.dtype)

    local_rot = pltpu.make_async_copy(rot, full.at[0, y, zl, c], loc.at[0])
    local_coef = pltpu.make_async_copy(coef, gath.at[x, zh], loc.at[1])

    peers = (right, left, *z_peers, *y_peers, twin)
    barrier = pltpu.get_barrier_semaphore()
    for dev in peers:
        pl.semaphore_signal(barrier, inc=1, device_id=dev, device_id_type=MESH)
    local_rot.start()
    pl.semaphore_wait(barrier, len(peers))

    over(0).start()
    for i in range(OWN_AHEAD):
        for d in range(2):
            own(i, d).start()
    for s in z_sends:
        s.start()
    for i in range(1, K_AHEAD):
        over(i).start()
    local_coef.start()
    local_rot.wait()
    local_coef.wait()

    def begin(t):
        return jnp.maximum(0, jnp.minimum(jnp.minimum(2 * (t - START), t - L_MULTIPLY), nb))

    def between(t, first, count, step=1):
        inside = jnp.logical_and(t >= first, t < first + step * count)
        return inside if step == 1 else jnp.logical_and(inside, lax.rem(t - first + step, step) == 0)

    steps = max(nb + L_MULTIPLY, FIRST_PAIR + 2 * nj - 1)

    @pl.loop(0, steps)
    def _(t):
        @pl.when(between(t, OWN_AHEAD, nb - OWN_AHEAD))
        def _():
            for d in range(2):
                own(t, d).start()

        @pl.when(between(t, 0, nb - K_AHEAD))
        def _():
            over(t + K_AHEAD).start()

        @pl.when(between(t, 0, nj))
        def _():
            for d in range(2):
                feed(t, d).start()
                pair_over(t, d).start()

        @pl.when(between(t, L_PARTNER, nb))
        def _():
            over(t - L_PARTNER).wait_recv()
            for d in range(2):
                partner(t - L_PARTNER, d).start()

        @pl.when(between(t, 2, nj))
        def _():
            for d in range(2):
                feed(t - 2, d).wait_recv()
                feeder_over(t - 2, d).start()

        @pl.when(between(t, L_FORWARD, nb))
        def _():
            for d in range(2):
                own(t - L_FORWARD, d).wait_recv()
                partner(t - L_FORWARD, d).wait_recv()
                forward(t - L_FORWARD, d).start()

        @pl.when(between(t, FIRST_MATE, nj, 2))
        def _():
            i = (t - FIRST_MATE) // 2
            for d in range(2):
                pair_over(i, d).wait_recv()
                mate_own(i, d).start()
            for d in range(2):
                feeder_over(i, d).wait_recv()
                mate_fed(i, d).start()

        @pl.when(t == ROT_1)
        def _():
            for s in z_sends:
                s.wait()
            for s in x_sends:
                s.start()
            for s in y_sends(0):
                s.start()

        @pl.when(t == ROT_2)
        def _():
            for s in x_sends:
                s.wait()
            for s in y_sends(1):
                s.start()

        @pl.when(t == ROT_3)
        def _():
            for s in y_sends(0):
                s.wait()
            c_send(0).start()

        @pl.when(t == START)
        def _():
            c_send(0).wait()

        @pl.when(t == ROT_4)
        def _():
            for s in y_sends(1):
                s.wait()
            c_send(1).start()

        @pl.when(t == ROT_5)
        def _():
            c_send(1).wait()

        @pl.loop(begin(t), begin(t + 1))
        def _(i):
            for d in range(2):
                forward(i, d).wait_recv()
            rows = rows_of(i, zh)
            prod[pl.ds(i * R, R), :] = times(rows, 1)
            product(i).start()
            out[rows, :] = times(rows, 0)

        @pl.when(between(t, FIRST_PAIR, nj, 2))
        def _():
            i = (t - FIRST_PAIR) // 2
            for d in range(2):
                mate_own(i, 1 - d).wait_recv()
                mate_fed(i, 1 - d).wait_recv()
                rows = pair_rows(i, pair[d])
                jprod[d, pl.ds(i * R, R), :] = times(rows, 2 + d)
                pair_product(i, d).start()
            for d in range(2):
                rows = pair_rows(i, pair[d])
                out[rows, :] = times(rows, 0)


    send(prod, prod, p_s, p_r, across).wait()
    for d in range(2):
        send(jprod.at[d], jprod.at[d], jo_s.at[d], jo_r.at[d], ways[d]).wait()

    def sent(s, blocks):
        ref = gath.at[0, 0, pl.ds(0, blocks * R)]
        send(ref, ref, s, p_r, across).wait_send()

    sent(k_s, nb)
    for d in range(2):
        for s in (own_s, par_s, fwd_s):
            sent(s.at[d], nb)
        for s in (feed_s, jk_s, jf_s):
            sent(s.at[d], nj)
        for s in (ma_s, mb_s):
            sent(s.at[d], 2 * nj)


def on_device(coeffs, rotation):
    coeffs, rotation = (pltpu.with_memory_space_constraint(v, pltpu.HBM) for v in (coeffs, rotation))
    rows, depth = coeffs.shape
    columns = rotation.shape[1]
    nj = NJ
    nb = (rows // R - 4 * nj) // 2
    dma = pltpu.SemaphoreType.DMA
    dtype = coeffs.dtype
    return pl.pallas_call(
        functools.partial(kernel, nb, nj),
        out_shape=pltpu.VMEM((rows, columns), dtype),
        in_specs=[pl.BlockSpec(memory_space=pltpu.HBM)] * 2,
        out_specs=pl.BlockSpec(memory_space=pltpu.VMEM),
        scratch_shapes=[
            pltpu.VMEM((4, 2, rows, depth), dtype),
            pltpu.VMEM((4, 4, 2, 2, rotation.shape[0], columns), dtype),
            pltpu.VMEM((nb * R, columns), dtype),
            pltpu.VMEM((2, nj * R, columns), dtype),
            dma((2,)), dma((2, nb)), dma((2,)), dma((2, nb)), dma((2,)), dma((2, nb)), dma, dma((nb,)), dma, dma,
            dma((2,)), dma((2, nj)), dma((2,)), dma((2, nj)), dma((2,)), dma((2, nj)),
            dma((2,)), dma((2, nj)), dma((2,)), dma((2, nj)), dma((2,)), dma((2,)),
            dma((3,)), dma((3,)), dma((2,)), dma((2,)), dma((2, 3)), dma((2, 3)), dma((2,)), dma((2,)), dma((2,)),
        ],
        compiler_params=pltpu.CompilerParams(
            collective_id=0, has_side_effects=True, vmem_limit_bytes=40 * 2**20
        ),
        cost_estimate=pl.CostEstimate(flops=2 * rows * 1024 * columns, bytes_accessed=rows * columns * 2, transcendentals=0),
    )(coeffs, rotation)


def solution(mesh):
    return jax.shard_map(
        on_device,
        mesh=mesh,
        in_specs=(P("gvec", "band"), P("gvec", "band")),
        out_specs=P("gvec", "band"),
        check_vma=False,
    )
```

time: 274 us -> 110 us (0.40)
  waiting for transfers between devices: 246 us -> 0 us
  Pallas kernels: 0 us -> 106 us
  matrix products: 14.7 us -> 0 us
  between operations: 13.4 us -> 0.01 us
  local copies, waits for them, and re-layouts: 0 us -> 3.4 us
    all_gather x2 -> x0, waiting for transfers between devices: 244 us -> none  [the longest x1 208 us: on_device(): whole = lax.all_gather(coeffs, 'band', axis=1, tiled=True)]
    pallas_call x0 -> x1, Pallas kernels: none -> 106 us  [on_device(): pl.pallas_call(functools.partial(kernel, nb, nj), out_shape=pltpu.VMEM((r...]
    dot_general x1 -> x0, matrix products: 14.7 us -> none  [on_device(): total = jnp.dot(whole, rows_full, preferred_element_type=jnp.float32)]
    unnamed x0 -> x1, local copies, waits for them, and re-layouts: none -> 3.4 us
  transfers between devices with their start and end apart: 2 -> 0, of which waited for: 2 -> 0; matrix products, arithmetic and copies ran while one was open for 0% -> 0% of each run, Pallas kernels for 0% -> 0%
where the time goes in v2:
time: 110 us; the launch traced here: 109 us
  Pallas kernels  106 us (96%)
  local copies, waits for them, and re-layouts  3.4 us (3%)
    pallas_call x1, Pallas kernels, on_device(): pl.pallas_call(functools.partial(kernel, nb, nj), out_shape=pltpu.VMEM((r...  106 us
    unnamed x1, local copies, waits for them, and re-layouts  3.4 us

profile of v2, /device:TPU:0, one launch (start us, length us, event | category | flops | bytes accessed | tf_op | source)
XLA Modules:
  0.0 109.5 jit_solution(11550659290345532519)
XLA Ops:
  0.0 106.1 %shard_map.28 = bf16[8192,512]{1,0:T(8,128)(2,1)S(1)} custom-call(bf16[8192,128]{1,0:T(8,128)(2,1)} %coef.1, bf16[64,512]{1,0:T(8,128)(2,1)} %rot.1), custom_call_target="tpu_custom_call" | custom-call | flops 8589934592 | bytes 8388608 | tf_op jit(solution)/shard_map/pallas_call | solution.py:275
  106.1 3.4 %copy.4 = bf16[8192,512]{1,0:T(8,128)(2,1)} copy(bf16[8192,512]{1,0:T(8,128)(2,1)S(1)} %shard_map.28) | data formatting | bytes 16777216

commit v3 on v2

--- a/solution.py
+++ b/solution.py
@@ -10,10 +10,10 @@
 MESH = pl.DeviceIdType.MESH
 R = 128
 NJ = 7
-K_AHEAD, OWN_AHEAD = 6, 4
-L_PARTNER, L_FORWARD, L_MULTIPLY = 3, 6, 9
-FIRST_MATE, FIRST_PAIR = 6, 11
-ROT_1, ROT_2, ROT_3, START, ROT_4, ROT_5 = 2, 4, 6, 7, 9, 10
+K_AHEAD, OWN_AHEAD = 11, 5
+L_PARTNER, L_FORWARD, L_MULTIPLY = 0, 5, 9
+L_FEED, FIRST_MATE, FIRST_PAIR, STRIDE = 2, 6, 14, 3
+ROT_1, ROT_2, ROT_3, START, ROT_4, ROT_5 = 1, 3, 6, 11, 12, 14
 
 
 def kernel(nb, nj, coef, rot, out, gath, full, prod, jprod, *sems):
@@ -139,7 +139,7 @@
         inside = jnp.logical_and(t >= first, t < first + step * count)
         return inside if step == 1 else jnp.logical_and(inside, lax.rem(t - first + step, step) == 0)
 
-    steps = max(nb + L_MULTIPLY, FIRST_PAIR + 2 * nj - 1)
+    steps = max(nb + L_MULTIPLY, FIRST_PAIR + STRIDE * (nj - 1) + 1)
 
     @pl.loop(0, steps)
     def _(t):
@@ -164,11 +164,11 @@
             for d in range(2):
                 partner(t - L_PARTNER, d).start()
 
-        @pl.when(between(t, 2, nj))
-        def _():
-            for d in range(2):
-                feed(t - 2, d).wait_recv()
-                feeder_over(t - 2, d).start()
+        @pl.when(between(t, L_FEED, nj))
+        def _():
+            for d in range(2):
+                feed(t - L_FEED, d).wait_recv()
+                feeder_over(t - L_FEED, d).start()
 
         @pl.when(between(t, L_FORWARD, nb))
         def _():
@@ -177,9 +177,9 @@
                 partner(t - L_FORWARD, d).wait_recv()
                 forward(t - L_FORWARD, d).start()
 
-        @pl.when(between(t, FIRST_MATE, nj, 2))
-        def _():
-            i = (t - FIRST_MATE) // 2
+        @pl.when(between(t, FIRST_MATE, nj, STRIDE))
+        def _():
+            i = (t - FIRST_MATE) // STRIDE
             for d in range(2):
                 pair_over(i, d).wait_recv()
                 mate_own(i, d).start()
@@ -232,9 +232,9 @@
             product(i).start()
             out[rows, :] = times(rows, 0)
 
-        @pl.when(between(t, FIRST_PAIR, nj, 2))
-        def _():
-            i = (t - FIRST_PAIR) // 2
+        @pl.when(between(t, FIRST_PAIR, nj, STRIDE))
+        def _():
+            i = (t - FIRST_PAIR) // STRIDE
             for d in range(2):
                 mate_own(i, 1 - d).wait_recv()
                 mate_fed(i, 1 - d).wait_recv()

time: 110 us -> 99.8 us (0.907)
  Pallas kernels: 106 us -> 96.3 us
    pallas_call x1, Pallas kernels: 106 us -> 96.3 us  [on_device(): pl.pallas_call(functools.partial(kernel, nb, nj), out_shape=pltpu.VMEM((r...]
where the time goes in v3:
time: 99.8 us; the launch traced here: 99.7 us
  Pallas kernels  96.3 us (96%)
  local copies, waits for them, and re-layouts  3.4 us (3%)
    pallas_call x1, Pallas kernels, on_device(): pl.pallas_call(functools.partial(kernel, nb, nj), out_shape=pltpu.VMEM((r...  96.3 us
    unnamed x1, local copies, waits for them, and re-layouts  3.4 us

profile of v3, /device:TPU:0, one launch (start us, length us, event | category | flops | bytes accessed | tf_op | source)
XLA Modules:
  0.0 99.7 jit_solution(2465691980011410958)
XLA Ops:
  0.0 96.3 %shard_map.28 = bf16[8192,512]{1,0:T(8,128)(2,1)S(1)} custom-call(bf16[8192,128]{1,0:T(8,128)(2,1)} %coef.1, bf16[64,512]{1,0:T(8,128)(2,1)} %rot.1), custom_call_target="tpu_custom_call" | custom-call | flops 8589934592 | bytes 8388608 | tf_op jit(solution)/shard_map/pallas_call | solution.py:275
  96.3 3.4 %copy.4 = bf16[8192,512]{1,0:T(8,128)(2,1)} copy(bf16[8192,512]{1,0:T(8,128)(2,1)S(1)} %shard_map.28) | data formatting | bytes 16777216

commit v4 on v3

--- a/solution.py
+++ b/solution.py
@@ -9,11 +9,11 @@
 
 MESH = pl.DeviceIdType.MESH
 R = 128
-NJ = 7
-K_AHEAD, OWN_AHEAD = 11, 5
-L_PARTNER, L_FORWARD, L_MULTIPLY = 0, 5, 9
-L_FEED, FIRST_MATE, FIRST_PAIR, STRIDE = 2, 6, 14, 3
-ROT_1, ROT_2, ROT_3, START, ROT_4, ROT_5 = 1, 3, 6, 11, 12, 14
+NJ, RJ = 6, 160
+K_AHEAD, OWN_AHEAD = 2, 5
+L_PARTNER, L_FORWARD, L_MULTIPLY = 3, 6, 10
+L_FEED, FIRST_MATE, FIRST_PAIR, STRIDE = 5, 10, 16, 2
+ROT_1, ROT_2, ROT_3, START, ROT_4, ROT_5 = 3, 7, 9, 11, 13, 14
 
 
 def kernel(nb, nj, coef, rot, out, gath, full, prod, jprod, *sems):
@@ -68,7 +68,7 @@
     fed = (xp, x2)
 
     def pair_rows(i, j):
-        return pl.ds(pl.multiple_of((2 * nb + j * nj + i) * R, R), R)
+        return pl.ds(pl.multiple_of(2 * nb * R + (j * nj + i) * RJ, 16), RJ)
 
     def feed(i, d):
         rows = pair_rows(i, fed[d])
@@ -91,7 +91,7 @@
         return send(ref, ref, mb_s.at[d], mb_r.at[d, i], ways[d])
 
     def pair_product(i, d):
-        return send(jprod.at[d, pl.ds(i * R, R)], out.at[pair_rows(i, pair[d])], jo_s.at[d], jo_r.at[d], ways[1 - d])
+        return send(jprod.at[d, pl.ds(i * RJ, RJ)], out.at[pair_rows(i, pair[d])], jo_s.at[d], jo_r.at[d], ways[1 - d])
 
 
     z_sends = [send(rot, full.at[(0, 1, 1)[k], y, zl, c], z_s.at[k], z_r.at[k], dev) for k, dev in enumerate(z_peers)]
@@ -239,7 +239,7 @@
                 mate_own(i, 1 - d).wait_recv()
                 mate_fed(i, 1 - d).wait_recv()
                 rows = pair_rows(i, pair[d])
-                jprod[d, pl.ds(i * R, R), :] = times(rows, 2 + d)
+                jprod[d, pl.ds(i * RJ, RJ), :] = times(rows, 2 + d)
                 pair_product(i, d).start()
             for d in range(2):
                 rows = pair_rows(i, pair[d])
@@ -250,18 +250,18 @@
     for d in range(2):
         send(jprod.at[d], jprod.at[d], jo_s.at[d], jo_r.at[d], ways[d]).wait()
 
-    def sent(s, blocks):
-        ref = gath.at[0, 0, pl.ds(0, blocks * R)]
+    def sent(s, rows):
+        ref = gath.at[0, 0, pl.ds(0, rows)]
         send(ref, ref, s, p_r, across).wait_send()
 
-    sent(k_s, nb)
+    sent(k_s, nb * R)
     for d in range(2):
         for s in (own_s, par_s, fwd_s):
-            sent(s.at[d], nb)
+            sent(s.at[d], nb * R)
         for s in (feed_s, jk_s, jf_s):
-            sent(s.at[d], nj)
+            sent(s.at[d], nj * RJ)
         for s in (ma_s, mb_s):
-            sent(s.at[d], 2 * nj)
+            sent(s.at[d], 2 * nj * RJ)
 
 
 def on_device(coeffs, rotation):
@@ -269,7 +269,7 @@
     rows, depth = coeffs.shape
     columns = rotation.shape[1]
     nj = NJ
-    nb = (rows // R - 4 * nj) // 2
+    nb = (rows - 4 * nj * RJ) // (2 * R)
     dma = pltpu.SemaphoreType.DMA
     dtype = coeffs.dtype
     return pl.pallas_call(
@@ -281,7 +281,7 @@
             pltpu.VMEM((4, 2, rows, depth), dtype),
             pltpu.VMEM((4, 4, 2, 2, rotation.shape[0], columns), dtype),
             pltpu.VMEM((nb * R, columns), dtype),
-            pltpu.VMEM((2, nj * R, columns), dtype),
+            pltpu.VMEM((2, nj * RJ, columns), dtype),
             dma((2,)), dma((2, nb)), dma((2,)), dma((2, nb)), dma((2,)), dma((2, nb)), dma, dma((nb,)), dma, dma,
             dma((2,)), dma((2, nj)), dma((2,)), dma((2, nj)), dma((2,)), dma((2, nj)),
             dma((2,)), dma((2, nj)), dma((2,)), dma((2, nj)), dma((2,)), dma((2,)),

time: 99.8 us -> 99.1 us (level)
  no operation moved by 1% of the time
where the time goes in v4:
time: 99.1 us; the launch traced here: 99 us
  Pallas kernels  95.6 us (96%)
  local copies, waits for them, and re-layouts  3.4 us (3%)
    pallas_call x1, Pallas kernels, on_device(): pl.pallas_call(functools.partial(kernel, nb, nj), out_shape=pltpu.VMEM((r...  95.6 us
    unnamed x1, local copies, waits for them, and re-layouts  3.4 us

profile of v4, /device:TPU:0, one launch (start us, length us, event | category | flops | bytes accessed | tf_op | source)
XLA Modules:
  0.0 99.0 jit_solution(11467395507703016171)
XLA Ops:
  0.0 95.6 %shard_map.28 = bf16[8192,512]{1,0:T(8,128)(2,1)S(1)} custom-call(bf16[8192,128]{1,0:T(8,128)(2,1)} %coef.1, bf16[64,512]{1,0:T(8,128)(2,1)} %rot.1), custom_call_target="tpu_custom_call" | custom-call | flops 8589934592 | bytes 8388608 | tf_op jit(solution)/shard_map/pallas_call | solution.py:275
  95.6 3.4 %copy.4 = bf16[8192,512]{1,0:T(8,128)(2,1)} copy(bf16[8192,512]{1,0:T(8,128)(2,1)S(1)} %shard_map.28) | data formatting | bytes 16777216

commit v5 on v4

--- a/solution.py
+++ b/solution.py
@@ -12,7 +12,7 @@
 NJ, RJ = 6, 160
 K_AHEAD, OWN_AHEAD = 2, 5
 L_PARTNER, L_FORWARD, L_MULTIPLY = 3, 6, 10
-L_FEED, FIRST_MATE, FIRST_PAIR, STRIDE = 5, 10, 16, 2
+L_FEED, FIRST_MATE, FIRST_PAIR, STRIDE = 5, 10, 15, 2
 ROT_1, ROT_2, ROT_3, START, ROT_4, ROT_5 = 3, 7, 9, 11, 13, 14
 
 

time: 99.1 us -> 99.6 us (level)
  no operation moved by 1% of the time
where the time goes in v5:
time: 99.6 us; the launch traced here: 99.4 us
  Pallas kernels  96 us (96%)
  local copies, waits for them, and re-layouts  3.4 us (3%)
    pallas_call x1, Pallas kernels, on_device(): pl.pallas_call(functools.partial(kernel, nb, nj), out_shape=pltpu.VMEM((r...  96 us
    unnamed x1, local copies, waits for them, and re-layouts  3.4 us

profile of v5, /device:TPU:0, one launch (start us, length us, event | category | flops | bytes accessed | tf_op | source)
XLA Modules:
  0.0 99.4 jit_solution(11216874196388408546)
XLA Ops:
  0.0 96.0 %shard_map.28 = bf16[8192,512]{1,0:T(8,128)(2,1)S(1)} custom-call(bf16[8192,128]{1,0:T(8,128)(2,1)} %coef.1, bf16[64,512]{1,0:T(8,128)(2,1)} %rot.1), custom_call_target="tpu_custom_call" | custom-call | flops 8589934592 | bytes 8388608 | tf_op jit(solution)/shard_map/pallas_call | solution.py:275
  96.0 3.4 %copy.4 = bf16[8192,512]{1,0:T(8,128)(2,1)} copy(bf16[8192,512]{1,0:T(8,128)(2,1)S(1)} %shard_map.28) | data formatting | bytes 16777216
